TPU v7x, 512 devices: a whole 4x4x16 slice. The times are simulated.
512 devices in a mesh: dp: 2 (over core), fsdp: 32 (over y, z_lo), tensor: 8 (over z_hi, x).
Axes of the slice: x: 4, y: 4, z: 16 (z_hi: 2, z_lo: 8; z = z_hi * 8 + z_lo), core: 2. Of those that a mesh axis runs over, the one named last changes fastest.
Arguments:
- tokens: bfloat16 [16384, 4096], P(('dp', 'fsdp', 'tensor')), may hold values from -40 to 40
- norm_gain: float32 [4096], replicated, may hold values from 0.5 to 1.5
- tile_values: bfloat16 [512, 128, 128], P(('fsdp', 'tensor')), may hold values from -0.25 to 0.25
- tile_rows: int32 [8, 64], P('tensor'), may hold values from 0 to 31, as said below
- tile_cols: int32 [8, 64], P('tensor'), may hold values from 0 to 13
- tile_counts: int32 [8, 32], P('tensor'), may hold values from 0 to 2, as said below
- grad_out: bfloat16 [16384, 14336], P(('dp', 'fsdp'), 'tensor'), may hold values from -3 to 3
Outputs:
- mixed: bfloat16 [16384, 14336], P(('dp', 'fsdp'), 'tensor')
- grad_x: bfloat16 [16384, 4096], P(('dp', 'fsdp', 'tensor'))
- grad_gain: float32 [4096], replicated
- grad_tiles: float32 [512, 128, 128], P(('fsdp', 'tensor'))
Inputs may be any that keep to these rules, and one draw needn't show every extreme that they name: `tile_counts`: for each tensor index the counts over the 32 fsdp shards sum to 56, and some shard holds exactly 2. `tile_rows`: within one tensor index the (row, column) pairs of held slots are all different.
All inputs are finite; a program needn't handle non-finite values.
Results may differ from a plain program's by a relative error of at most 0.013.
Values may be sent and summed in bfloat16 or wider, within the bound.
A program may use at most 128 MiB of HBM per device.

v0:
```python
import jax
import jax.numpy as jnp
from jax import lax
from jax.sharding import PartitionSpec as P


def tile_forward(group_rows, values, rows_list, cols_list, col_tiles):
    tile_size = values.shape[1]
    blocks = group_rows.reshape(group_rows.shape[0], -1, tile_size)
    picked = jnp.take(blocks, rows_list, axis=1)
    product = jnp.einsum("tsk,skn->tsn", picked, values, preferred_element_type=jnp.float32)
    placed = (
        jnp.zeros((group_rows.shape[0], col_tiles, tile_size), jnp.float32)
        .at[:, cols_list]
        .add(product)
    )
    return placed.reshape(group_rows.shape[0], col_tiles * tile_size)


def tile_backward(grad_rows, values, rows_list, cols_list, row_tiles):
    tile_size = values.shape[1]
    blocks = grad_rows.reshape(grad_rows.shape[0], -1, tile_size)
    picked = jnp.take(blocks, cols_list, axis=1)
    product = jnp.einsum("tsn,skn->tsk", picked, values, preferred_element_type=jnp.float32)
    placed = (
        jnp.zeros((grad_rows.shape[0], row_tiles, tile_size), jnp.float32)
        .at[:, rows_list]
        .add(product)
    )
    return placed.reshape(grad_rows.shape[0], row_tiles * tile_size)


def per_device(tokens, norm_gain, tile_values, tile_rows, tile_cols, tile_counts, grad_out):
    tile_size = tile_values.shape[1]
    slot_cap = tile_values.shape[0]
    row_tiles = tokens.shape[1] // tile_size
    col_tiles = grad_out.shape[1] // tile_size
    rows_list = tile_rows[0]
    cols_list = tile_cols[0]
    shard_counts = tile_counts[0]
    held_all = (jnp.arange(slot_cap)[None, :] < shard_counts[:, None]).reshape(-1)
    own_held = jnp.arange(slot_cap) < shard_counts[lax.axis_index("fsdp")]
    local_float = tokens.astype(jnp.float32)
    inv_rms = lax.rsqrt(jnp.mean(local_float * local_float, axis=1, keepdims=True) + 1e-05)
    scaled = local_float * inv_rms
    normed = (scaled * norm_gain).astype(jnp.bfloat16)
    group_rows = lax.all_gather(normed, "tensor", axis=0, tiled=True)
    gathered = lax.all_gather(tile_values, "fsdp", axis=0, tiled=True)
    kept_values = jnp.where(held_all[:, None, None], gathered, jnp.zeros_like(gathered))
    outputs = tile_forward(group_rows, kept_values, rows_list, cols_list, col_tiles)
    mixed = outputs.astype(jnp.bfloat16)
    input_grad = lax.psum_scatter(
        tile_backward(grad_out, kept_values, rows_list, cols_list, row_tiles).astype(jnp.bfloat16),
        "tensor",
        scatter_dimension=0,
        tiled=True,
    ).astype(jnp.float32)
    x_blocks = group_rows.reshape(group_rows.shape[0], row_tiles, tile_size)
    g_blocks = grad_out.reshape(grad_out.shape[0], col_tiles, tile_size)
    picked_x = jnp.take(x_blocks, rows_list, axis=1)
    picked_g = jnp.take(g_blocks, cols_list, axis=1)
    grad_shard = lax.psum_scatter(
        jnp.einsum("tsk,tsn->skn", picked_x, picked_g, preferred_element_type=jnp.float32),
        "fsdp",
        scatter_dimension=0,
        tiled=True,
    )
    grad_shard = jnp.where(own_held[:, None, None], grad_shard, jnp.zeros_like(grad_shard))
    grad_tiles = lax.psum(grad_shard, "dp")
    gain_part = jnp.sum(input_grad * scaled, axis=0)
    grad_gain = lax.psum(gain_part, ("dp", "fsdp", "tensor"))
    hidden_grad = input_grad * norm_gain
    grad_x = (
        inv_rms * (hidden_grad - scaled * jnp.mean(hidden_grad * scaled, axis=1, keepdims=True))
    ).astype(jnp.bfloat16)
    return (mixed, grad_x, grad_gain, grad_tiles)


def solution(mesh):
    placed = (
        P(("dp", "fsdp", "tensor"), None),
        P(),
        P(("fsdp", "tensor"), None, None),
        P("tensor", None),
        P("tensor", None),
        P("tensor", None),
        P(("dp", "fsdp"), "tensor"),
    )
    return jax.shard_map(
        per_device,
        mesh=mesh,
        in_specs=placed,
        out_specs=(
            P(("dp", "fsdp"), "tensor"),
            P(("dp", "fsdp", "tensor"), None),
            P(),
            P(("fsdp", "tensor"), None, None),
        ),
        check_vma=False,
    )
```

profile of v0, /device:TPU:1, one launch (start us, length us, event | category | flops | bytes accessed | tf_op | source)
XLA Modules:
  0.0 848.5 jit_solution(9026113694259479338)
XLA Ops:
  7.9 1.5 copy.32
  11.6 3.1 gather_fusion.1
  14.7 207.7 %all-gather.3.cloned.1.call-done = bf16[64,128,128]{2,1,0:T(8,128)(2,1)} async-done(((bf16[2,128,128]{2,1,0:T(8,128)(2,1)}), bf16[64,128,128]{2,1,0:T(8,128)(2,1)}) %all-gather.3.cloned.1.call-update) | async-done | bytes 2097168 | tf_op jit(solution)/shard_map/all_gather | solution.py:48
  222.3 7.4 fusion.2
  229.8 2.4 broadcast_in_dim.57
  232.2 19.4 %scatter_fusion.1 = f32[256,32,128]{2,0,1:T(8,128)} fusion(f32[256,32,128]{2,0,1:T(8,128)} %broadcast_in_dim.57, s32[64]{0:T(128)S(1)} %fusion.18, f32[64,256,128]{2,1,0:T(8,128)} %fusion.2), kind=kCustom, calls=%fused_computation.3 | custom fusion | flops 2097152 | bytes 25166080 | tf_op jit(solution)/shard_map/scatter-add | solution.py:28
  251.6 2.5 convert_element_type.28
  254.1 2.9 copy.34
  257.0 4.1 copy.39
  261.4 162.8 %reduce-scatter.7.cloned.1.call-done = bf16[32,4096]{1,0:T(8,128)(2,1)} async-done(((bf16[256,4096]{1,0:T(8,128)(2,1)}), bf16[32,4096]{1,0:T(8,128)(2,1)}) %reduce-scatter.7.cloned.1.call-update) | async-done | bytes 262160 | tf_op jit(solution)/shard_map/reduce_scatter | solution.py:52
  425.5 1.9 fusion.12
  427.6 109.9 %all-gather.5.cloned.1.call-done = bf16[256,4096]{1,0:T(8,128)(2,1)} async-done(((bf16[32,4096]{1,0:T(8,128)(2,1)}), bf16[256,4096]{1,0:T(8,128)(2,1)}) %all-gather.5.cloned.1.call-update) | async-done | bytes 2097168 | tf_op jit(solution)/shard_map/all_gather | solution.py:47
  537.5 4.1 copy.29
  541.6 3.2 copy.30
  544.8 3.0 gather_fusion
  547.8 7.0 fusion
  556.7 103.2 %psum.14 = f32[4096]{0:T(1024)} all-reduce(f32[4096]{0:T(1024)S(1)} %get-tuple-element.18), channel_id=1, replica_groups=mesh['dp'=2,'fsdp'=32,'tensor'=8] {'dp','fsdp','tensor'}, use_global_device_ids=true, to_apply=%region_6.9 | all-reduce | flops 4096 | bytes 32768 | tf_op jit(solution)/shard_map/psum | solution.py:71
  659.9 119.5 %reduce-scatter.5.cloned.1.call-done = f32[2,128,128]{2,1,0:T(8,128)} async-done(((f32[64,128,128]{2,1,0:T(8,128)}), f32[2,128,128]{2,1,0:T(8,128)}) %reduce-scatter.5.cloned.1.call-update) | async-done | bytes 131088 | tf_op jit(solution)/shard_map/reduce_scatter | solution.py:62
  779.5 1.6 broadcast_select_fusion.9
  781.1 6.7 fusion.5
  788.0 12.4 %scatter_fusion = f32[256,14,128]{2,0,1:T(8,128)S(1)} fusion(f32[256,14,128]{2,0,1:T(8,128)S(1)} %broadcast_in_dim.54, s32[64]{0:T(128)S(1)} %fusion.17, f32[64,256,128]{2,1,0:T(8,128)} %fusion.5), kind=kCustom, calls=%fused_computation.2 | custom fusion | flops 2097152 | bytes 25166080 | tf_op jit(solution)/shard_map/scatter-add | solution.py:15
  801.2 1.4 copy.37
  802.5 37.8 %all-reduce.2.cloned.1.call-done = f32[2,128,128]{2,1,0:T(8,128)} async-done(((f32[2,128,128]{2,1,0:T(8,128)}), f32[2,128,128]{2,1,0:T(8,128)}) %all-reduce.2.cloned.1.call-update) | async-done | bytes 131088 | tf_op jit(solution)/shard_map/psum | solution.py:69
  840.4 1.6 copy.44
  (41 shorter events, 7.2 us)
Async XLA Ops:
  7.2 215.2 %all-gather.3.cloned.1.call-start = ((), (), s32[]{:S(2)}) async-start(), calls=%async_computation.2 | async-start | bytes 2162688 | tf_op jit(solution)/shard_map/all_gather | solution.py:48
  7.9 416.4 %reduce-scatter.7.cloned.1.call-start = ((), (), s32[]{:S(2)}) async-start(), calls=%async_computation.6 | async-start | bytes 2359296 | tf_op jit(solution)/shard_map/reduce_scatter | solution.py:52
  11.6 3.1 copy-start.4
  11.6 3.1 copy-start.5
  257.0 4.2 copy-start.1
  257.0 167.2 %copy-start.2 = (f32[4096]{0:T(1024)S(1)}, f32[4096]{0:T(1024)}, u32[]{:S(2)}) copy-start(f32[4096]{0:T(1024)} %param.12) | copy-start | bytes 49156
  261.2 276.3 %all-gather.5.cloned.1.call-start = ((), (), s32[]{:S(2)}) async-start(), calls=%async_computation.3 | async-start | bytes 2359296 | tf_op jit(solution)/shard_map/all_gather | solution.py:47
  427.5 352.0 %reduce-scatter.5.cloned.1.call-start = ((), (), s32[]{:S(2)}) async-start(), calls=%async_computation.4 | async-start | bytes 4325376 | tf_op jit(solution)/shard_map/reduce_scatter | solution.py:62
  554.8 0.7 copy-start.3
  554.8 226.3 %copy-start = (bf16[64,128,128]{2,1,0:T(8,128)(2,1)S(1)}, bf16[64,128,128]{2,1,0:T(8,128)(2,1)}, u32[]{:S(2)}) copy-start(bf16[64,128,128]{2,1,0:T(8,128)(2,1)} %all-gather.3.cloned.1.call-done) | copy-start | bytes 6291460
  554.9 285.5 %all-reduce.2.cloned.1.call-start = ((), (), s32[]{:S(2)}) async-start(), calls=%async_computation.5 | async-start | bytes 262144 | tf_op jit(solution)/shard_map/psum | solution.py:69
Sparse Core Ops, SparseCore 0:
  10.1 212.2 all-gather.2
  261.3 162.8 reduce-scatter.6
  428.5 108.9 all-gather.4
  555.0 224.4 reduce-scatter.4
  783.0 57.3 all-reduce.1
where the time goes:
time: 849 us; the launch traced here: 848 us
  waiting for transfers between devices  639 us (75%)
  blocking collectives  103 us (12%)
  other arithmetic  41.6 us (5%)
  local copies, waits for them, and re-layouts  29.9 us (4%)
  matrix products  21.2 us (2%)
  between operations  13.9 us (2%)
    all_gather x1, waiting for transfers between devices, per_device(): gathered = lax.all_gather(tile_values, 'fsdp', axis=0, tiled=True)  208 us
    reduce_scatter x1, waiting for transfers between devices, per_device(): lax.psum_scatter(tile_backward(grad_out, kept_values, rows_list, cols_lis...  163 us
    reduce_scatter x1, waiting for transfers between devices, per_device(): lax.psum_scatter(jnp.einsum('tsk,tsn->skn', picked_x, picked_g, preferred...  120 us
    all_gather x1, waiting for transfers between devices, per_device(): group_rows = lax.all_gather(normed, 'tensor', axis=0, tiled=True)  110 us
    psum x1, blocking collectives, per_device(): grad_gain = lax.psum(gain_part, ('dp', 'fsdp', 'tensor'))  103 us
    psum x1, waiting for transfers between devices, per_device(): grad_tiles = lax.psum(grad_shard, 'dp')  37.8 us
    scatter-add x1, other arithmetic, tile_backward(): placed = jnp.zeros((grad_rows.shape[0], row_tiles, tile_size), jnp.float3...  19.4 us
  transfers between devices with their start and end apart: 5, of which 5 were waited for; matrix products, arithmetic and copies ran while one was open for 3% of the time, Pallas kernels for 0%

commit v1 on v0

--- a/solution.py
+++ b/solution.py
@@ -66,7 +66,8 @@
         tiled=True,
     )
     grad_shard = jnp.where(own_held[:, None, None], grad_shard, jnp.zeros_like(grad_shard))
-    grad_tiles = lax.psum(grad_shard, "dp")
+    shards = lax.all_gather(grad_shard, "dp", axis=0, tiled=False)
+    grad_tiles = shards.sum(axis=0)
     gain_part = jnp.sum(input_grad * scaled, axis=0)
     grad_gain = lax.psum(gain_part, ("dp", "fsdp", "tensor"))
     hidden_grad = input_grad * norm_gain

time: 849 us -> 817 us (0.962)
  waiting for transfers between devices: 639 us -> 580 us
  blocking collectives: 103 us -> 131 us
    psum x1 -> x0, waiting for transfers between devices: 37.8 us -> none  [per_device(): grad_tiles = lax.psum(grad_shard, 'dp')]
    all_gather x0 -> x1, blocking collectives: none -> 27.3 us  [per_device(): shards = lax.all_gather(grad_shard, 'dp', axis=0, tiled=False)]
    reduce_scatter x1, waiting for transfers between devices: 120 us -> 98.2 us  [per_device(): lax.psum_scatter(jnp.einsum('tsk,tsn->skn', picked_x, picked_g, preferred...]
  transfers between devices with their start and end apart: 5 -> 4, of which waited for: 5 -> 4; matrix products, arithmetic and copies ran while one was open for 3% -> 4% of each run, Pallas kernels for 0% -> 0%
where the time goes in v1:
time: 817 us; the launch traced here: 816 us
  waiting for transfers between devices  580 us (71%)
  blocking collectives  131 us (16%)
  other arithmetic  41.6 us (5%)
  local copies, waits for them, and re-layouts  28.4 us (3%)
  matrix products  21.2 us (3%)
  between operations  13.9 us (2%)
    all_gather x1, waiting for transfers between devices, per_device(): gathered = lax.all_gather(tile_values, 'fsdp', axis=0, tiled=True)  208 us
    reduce_scatter x1, waiting for transfers between devices, per_device(): lax.psum_scatter(tile_backward(grad_out, kept_values, rows_list, cols_lis...  164 us
    all_gather x1, waiting for transfers between devices, per_device(): group_rows = lax.all_gather(normed, 'tensor', axis=0, tiled=True)  110 us
    psum x1, blocking collectives, per_device(): grad_gain = lax.psum(gain_part, ('dp', 'fsdp', 'tensor'))  103 us
    reduce_scatter x1, waiting for transfers between devices, per_device(): lax.psum_scatter(jnp.einsum('tsk,tsn->skn', picked_x, picked_g, preferred...  98.2 us
    all_gather x1, blocking collectives, per_device(): shards = lax.all_gather(grad_shard, 'dp', axis=0, tiled=False)  27.3 us
    scatter-add x1, other arithmetic, tile_backward(): placed = jnp.zeros((grad_rows.shape[0], row_tiles, tile_size), jnp.float3...  19.4 us
  transfers between devices with their start and end apart: 4, of which 4 were waited for; matrix products, arithmetic and copies ran while one was open for 4% of the time, Pallas kernels for 0%

profile of v1, /device:TPU:1, one launch (start us, length us, event | category | flops | bytes accessed | tf_op | source)
XLA Modules:
  0.0 815.9 jit_solution(13245853512142414644)
XLA Ops:
  7.9 1.5 copy.32
  11.6 3.1 gather_fusion.1
  14.7 207.7 %all-gather.4.cloned.1.call-done = bf16[64,128,128]{2,1,0:T(8,128)(2,1)} async-done(((bf16[2,128,128]{2,1,0:T(8,128)(2,1)}), bf16[64,128,128]{2,1,0:T(8,128)(2,1)}) %all-gather.4.cloned.1.call-update) | async-done | bytes 2097168 | tf_op jit(solution)/shard_map/all_gather | solution.py:48
  222.3 7.4 fusion.2
  229.8 2.4 broadcast_in_dim.57
  232.2 19.4 %scatter_fusion.1 = f32[256,32,128]{2,0,1:T(8,128)} fusion(f32[256,32,128]{2,0,1:T(8,128)} %broadcast_in_dim.57, s32[64]{0:T(128)S(1)} %fusion.18, f32[64,256,128]{2,1,0:T(8,128)} %fusion.2), kind=kCustom, calls=%fused_computation.3 | custom fusion | flops 2097152 | bytes 25166080 | tf_op jit(solution)/shard_map/scatter-add | solution.py:28
  251.6 2.5 convert_element_type.28
  254.1 2.9 copy.34
  257.0 4.2 copy.39
  261.4 163.5 %reduce-scatter.7.cloned.1.call-done = bf16[32,4096]{1,0:T(8,128)(2,1)} async-done(((bf16[256,4096]{1,0:T(8,128)(2,1)}), bf16[32,4096]{1,0:T(8,128)(2,1)}) %reduce-scatter.7.cloned.1.call-update) | async-done | bytes 262160 | tf_op jit(solution)/shard_map/reduce_scatter | solution.py:52
  425.0 1.3 fusion.16
  426.3 1.9 fusion.12
  428.3 109.9 %all-gather.6.cloned.1.call-done = bf16[256,4096]{1,0:T(8,128)(2,1)} async-done(((bf16[32,4096]{1,0:T(8,128)(2,1)}), bf16[256,4096]{1,0:T(8,128)(2,1)}) %all-gather.6.cloned.1.call-update) | async-done | bytes 2097168 | tf_op jit(solution)/shard_map/all_gather | solution.py:47
  538.2 4.1 copy.29
  542.2 3.2 copy.30
  545.5 3.0 gather_fusion
  548.5 7.0 fusion
  557.4 103.3 %psum.7 = f32[4096]{0:T(1024)} all-reduce(f32[4096]{0:T(1024)S(1)} %get-tuple-element.18), channel_id=1, replica_groups=mesh['dp'=2,'fsdp'=32,'tensor'=8] {'dp','fsdp','tensor'}, use_global_device_ids=true, to_apply=%region_6.9 | all-reduce | flops 4096 | bytes 32768 | tf_op jit(solution)/shard_map/psum | solution.py:72
  660.7 6.7 fusion.5
  667.6 12.4 %scatter_fusion = f32[256,14,128]{2,0,1:T(8,128)S(1)} fusion(f32[256,14,128]{2,0,1:T(8,128)S(1)} %broadcast_in_dim.54, s32[64]{0:T(128)S(1)} %fusion.17, f32[64,256,128]{2,1,0:T(8,128)} %fusion.5), kind=kCustom, calls=%fused_computation.2 | custom fusion | flops 2097152 | bytes 25166080 | tf_op jit(solution)/shard_map/scatter-add | solution.py:15
  680.8 1.4 copy.37
  682.2 98.2 %reduce-scatter.5.cloned.1.call-done = f32[2,128,128]{2,1,0:T(8,128)} async-done(((f32[64,128,128]{2,1,0:T(8,128)}), f32[2,128,128]{2,1,0:T(8,128)}) %reduce-scatter.5.cloned.1.call-update) | async-done | bytes 131088 | tf_op jit(solution)/shard_map/reduce_scatter | solution.py:62
  780.4 1.0 broadcast_select_fusion.9
  781.4 27.3 %all-gather = f32[4,128,128]{2,1,0:T(8,128)S(1)} all-gather(f32[2,128,128]{2,1,0:T(8,128)S(1)} %broadcast_select_fusion.9), channel_id=2, replica_groups=mesh['dp'=2,'fsdp'=32,'tensor'=8] {'dp'}, dimensions={0}, use_global_device_ids=true | all-gather | bytes 393216 | tf_op jit(solution)/shard_map/all_gather | solution.py:69
  (39 shorter events, 6.6 us)
Async XLA Ops:
  7.2 215.2 %all-gather.4.cloned.1.call-start = ((), (), s32[]{:S(2)}) async-start(), calls=%async_computation.2 | async-start | bytes 2162688 | tf_op jit(solution)/shard_map/all_gather | solution.py:48
  7.9 417.1 %reduce-scatter.7.cloned.1.call-start = ((), (), s32[]{:S(2)}) async-start(), calls=%async_computation.5 | async-start | bytes 2359296 | tf_op jit(solution)/shard_map/reduce_scatter | solution.py:52
  11.6 3.1 copy-start.4
  11.6 3.1 copy-start.5
  257.0 4.2 copy-start.1
  257.0 168.0 %copy-start.2 = (f32[4096]{0:T(1024)S(1)}, f32[4096]{0:T(1024)}, u32[]{:S(2)}) copy-start(f32[4096]{0:T(1024)} %param.12) | copy-start | bytes 49156
  261.2 277.0 %all-gather.6.cloned.1.call-start = ((), (), s32[]{:S(2)}) async-start(), calls=%async_computation.3 | async-start | bytes 2359296 | tf_op jit(solution)/shard_map/all_gather | solution.py:47
  428.2 352.1 %reduce-scatter.5.cloned.1.call-start = ((), (), s32[]{:S(2)}) async-start(), calls=%async_computation.4 | async-start | bytes 4325376 | tf_op jit(solution)/shard_map/reduce_scatter | solution.py:62
  555.5 0.7 copy-start.3
  555.5 105.2 %copy-start = (bf16[64,128,128]{2,1,0:T(8,128)(2,1)S(1)}, bf16[64,128,128]{2,1,0:T(8,128)(2,1)}, u32[]{:S(2)}) copy-start(bf16[64,128,128]{2,1,0:T(8,128)(2,1)} %all-gather.4.cloned.1.call-done) | copy-start | bytes 6291460
Sparse Core Ops, SparseCore 0:
  10.1 212.2 all-gather.3
  261.3 163.6 reduce-scatter.6
  429.3 108.8 all-gather.5
  555.7 224.6 reduce-scatter.4
